TPU v7x, 32 devices: a whole 2x2x4 slice. The times are simulated.
32 devices in a mesh: dp: 8 (over z, core), group: 4 (over y, x).
Axes of the slice: x: 2, y: 2, z: 4, core: 2. Of those that a mesh axis runs over, the one named last changes fastest.
Arguments:
- attended: bfloat16 [16384, 768], P(('dp', 'group')), may hold values from -6 to 6
- cotangent: bfloat16 [16384, 1536], P(('dp', 'group')), may hold values from -6 to 6
- weight: float32 [768, 1536], P('dp'), may hold values from -0.21875 to 0.21875
- weight_first: float32 [768, 1536], P('dp'), may hold values from -0.0078125 to 0.0078125, as said below
- weight_second: float32 [768, 1536], P('dp'), may hold values from 2.44140625e-09 to 1.2207031e-06, as said below
- bias: float32 [1536], replicated, may hold values from -3 to 3
- layer_scale: float32 [1536], replicated, may hold values from 0.1 to 1, as said below
- small_first: float32 [2, 1536], replicated, may hold values from -0.0078125 to 0.0078125, as said below
- small_second: float32 [2, 1536], replicated, may hold values from 2.44140625e-09 to 1.2207031e-06, as said below
- teacher_weight: float32 [768, 1536], P('dp'), may hold values from -0.21875 to 0.21875
- teacher_bias: float32 [1536], replicated, may hold values from -3 to 3
- teacher_scale: float32 [1536], replicated, may hold values from 0.1 to 1
- teacher_attended: bfloat16 [4096, 768], P(('dp', 'group')), may hold values from -6 to 6
- teacher_resid: bfloat16 [4096, 1536], P(('dp', 'group')), may hold values from -6 to 6
Outputs:
- new_weight: float32 [768, 1536], P('dp')
- new_weight_first: float32 [768, 1536], P('dp')
- new_weight_second: float32 [768, 1536], P('dp')
- weight_direction: float32 [768, 1536], P('dp')
- new_teacher_weight: float32 [768, 1536], P('dp')
- new_small: float32 [2, 1536], replicated
- new_small_first: float32 [2, 1536], replicated
- new_small_second: float32 [2, 1536], replicated
- small_direction: float32 [2, 1536], replicated
- new_teacher_small: float32 [2, 1536], replicated
- teacher_out: bfloat16 [4096, 1536], P(('dp', 'group'))
Inputs may be any that keep to these rules, and one draw needn't show every extreme that they name: `layer_scale`: LayerScale factors of a trained block. `weight_first`: moment estimates of an Adam state. `weight_second`: moment estimates of an Adam state. `small_first`: moment estimates of an Adam state. `small_second`: moment estimates of an Adam state.
All inputs are finite; a program needn't handle non-finite values.
Results may differ from a plain program's by a relative error of at most 0.0085.
Values may be sent and summed in bfloat16 or wider, within the bound.
A program may use at most 64 MiB of HBM per device.

v0:
```python
import jax
import jax.numpy as jnp
from jax import lax
from jax.sharding import PartitionSpec as P

BETA_ONE = 0.9
BETA_TWO = 0.999
LEARN_RATE = 0.0004
WEIGHT_DECAY = 0.04
EPSILON = 1e-08
MOMENTUM = 0.994
CORRECT_ONE = 1.0 - 0.9**10
CORRECT_TWO = 1.0 - 0.999**10


def adam_update(param, first, second, grad, decay):
    first = BETA_ONE * first + (1.0 - BETA_ONE) * grad
    second = BETA_TWO * second + (1.0 - BETA_TWO) * grad * grad
    direction = first / CORRECT_ONE / (jnp.sqrt(second / CORRECT_TWO) + EPSILON) + decay * param
    return (param - LEARN_RATE * direction, first, second, direction)


def local(
    attended,
    cotangent,
    weight,
    weight_first,
    weight_second,
    bias,
    layer_scale,
    small_first,
    small_second,
    teacher_weight,
    teacher_bias,
    teacher_scale,
    teacher_attended,
    teacher_resid,
):
    total = attended.shape[0] * lax.axis_size("dp") * lax.axis_size("group")
    grad_rows = cotangent.astype(jnp.float32)
    bias_part = jnp.sum(grad_rows, 0)
    inputs = attended
    shard_part = lax.psum_scatter(
        lax.dot_general(
            inputs, cotangent, (((0,), (0,)), ((), ())), preferred_element_type=jnp.float32
        ).astype(jnp.bfloat16),
        "dp",
        scatter_dimension=0,
        tiled=True,
    )
    narrow = weight.astype(jnp.bfloat16)
    inputs = attended
    projected = jnp.dot(
        inputs, lax.all_gather(narrow, "dp", axis=0, tiled=True), preferred_element_type=jnp.float32
    )
    scale_part = jnp.sum(grad_rows * (projected + bias), 0)
    bias_sum, scale_sum = lax.psum((bias_part, scale_part), ("dp", "group"))
    summed = lax.psum(shard_part, "group").astype(jnp.float32)
    grad_weight = summed * layer_scale[None, :] / total
    grad_small = jnp.stack([layer_scale * bias_sum, scale_sum]) / total
    new_weight, new_weight_first, new_weight_second, weight_direction = adam_update(
        weight, weight_first, weight_second, grad_weight, WEIGHT_DECAY
    )
    small = jnp.stack([bias, layer_scale])
    new_small, new_small_first, new_small_second, small_direction = adam_update(
        small, small_first, small_second, grad_small, 0.0
    )
    new_teacher_weight = MOMENTUM * teacher_weight + (1.0 - MOMENTUM) * weight
    new_teacher_small = (
        MOMENTUM * jnp.stack([teacher_bias, teacher_scale]) + (1.0 - MOMENTUM) * small
    )
    inputs = teacher_attended
    teacher_branch = jnp.dot(
        inputs,
        lax.all_gather(new_teacher_weight.astype(jnp.bfloat16), "dp", axis=0, tiled=True),
        preferred_element_type=jnp.float32,
    )
    teacher_out = (
        teacher_resid.astype(jnp.float32)
        + new_teacher_small[1] * (teacher_branch + new_teacher_small[0])
    ).astype(jnp.bfloat16)
    return (
        new_weight,
        new_weight_first,
        new_weight_second,
        weight_direction,
        new_teacher_weight,
        new_small,
        new_small_first,
        new_small_second,
        small_direction,
        new_teacher_small,
        teacher_out,
    )


def solution(mesh):
    placed = (
        P(("dp", "group"), None),
        P(("dp", "group"), None),
        P("dp", None),
        P("dp", None),
        P("dp", None),
        P(),
        P(),
        P(),
        P(),
        P("dp", None),
        P(),
        P(),
        P(("dp", "group"), None),
        P(("dp", "group"), None),
    )
    return jax.shard_map(
        local,
        mesh=mesh,
        in_specs=placed,
        out_specs=(
            P("dp", None),
            P("dp", None),
            P("dp", None),
            P("dp", None),
            P("dp", None),
            P(),
            P(),
            P(),
            P(),
            P(),
            P(("dp", "group"), None),
        ),
        check_vma=False,
    )
```

profile of v0, /device:TPU:0, one launch (start us, length us, event | category | flops | bytes accessed | tf_op | source)
XLA Modules:
  0.0 187.4 jit_solution(16931490593272864425)
XLA Ops:
  7.2 0.0 copy-start
  7.2 0.0 reduce-scatter.2.cloned.1.call-start
  7.2 1.1 copy-done
  8.3 4.2 %convolution_convert_fusion = bf16[768,1536]{1,0:T(8,128)(2,1)} fusion(bf16[512,768]{1,0:T(8,128)(2,1)S(1)} %copy-done, bf16[512,1536]{1,0:T(8,128)(2,1)} %param.15), kind=kOutput, calls=%fused_computation.2 | convolution fusion | flops 1209139200 | bytes 4718592 | tf_op jit(solution)/shard_map/dot_general | solution.py:44
  12.6 0.0 reduce-scatter.2.cloned.1.call-update
  12.6 0.0 all-reduce.3.cloned.1.call-start
  12.6 39.2 %reduce-scatter.2.cloned.1.call-done = bf16[96,1536]{1,0:T(8,128)(2,1)} async-done(((bf16[768,1536]{1,0:T(8,128)(2,1)}), bf16[96,1536]{1,0:T(8,128)(2,1)}) %reduce-scatter.2.cloned.1.call-update) | async-done | bytes 294928 | tf_op jit(solution)/shard_map/reduce_scatter | solution.py:43
  51.8 0.0 all-reduce.3.cloned.1.call-update
  51.8 0.0 copy-start.8
  51.8 0.0 copy-start.1
  51.8 0.0 all-gather.3.cloned.1.call-start
  51.9 45.3 %all-reduce.3.cloned.1.call-done = bf16[96,1536]{1,0:T(8,128)(2,1)} async-done(((bf16[96,1536]{1,0:T(8,128)(2,1)}), bf16[96,1536]{1,0:T(8,128)(2,1)}) %all-reduce.3.cloned.1.call-update) | async-done | bytes 294928 | tf_op jit(solution)/shard_map/psum | solution.py:58
  97.2 0.0 copy-done.4
  97.2 3.3 %fusion.6 = (bf16[96,1536]{1,0:T(8,128)(2,1)}, f32[96,1536]{1,0:T(8,128)}, bf16[96,1536]{1,0:T(8,128)(2,1)}, f32[96,1536]{1,0:T(8,128)}, f32[96,1536]{1,0:T(8,128)}, /*index=5*/f32[96,1536]{1,0:T(8,128)}, f32[96,1536]{1,0:T(8,128)}) fusion(f32[96,1536]{1,0:T(8,128)S(1)} %copy-done.2, f32[96,1536]{1,0:T(8,128)S(1)} %copy-done.3, f32[96,1536]{1,0:T(8,128)} %param.18, ...), kind=kLoop, calls=%fused_computation.26 | loop fusion | flops 3391488 | bytes 6199296 | tf_op jit(solution)/shard_map/convert_element_type | solution.py:75
  100.5 0.0 all-gather.3.cloned.1.call-update
  100.5 0.0 all-gather.5.cloned.1.call-start
  100.5 0.5 all-gather.5.cloned.1.call-update
  101.1 0.7 stack.25
  101.8 0.7 stack.31
  102.5 1.2 copy.25
  103.7 0.3 convert_reduce_fusion
  104.0 0.0 copy-start.7
  104.0 0.0 copy-start.10
  104.0 28.2 %all-gather.3.cloned.1.call-done = bf16[768,1536]{1,0:T(8,128)(2,1)} async-done(((bf16[96,1536]{1,0:T(8,128)(2,1)}), bf16[768,1536]{1,0:T(8,128)(2,1)}) %all-gather.3.cloned.1.call-update) | async-done | bytes 2359312 | tf_op jit(solution)/shard_map/all_gather | solution.py:54
  132.3 3.1 %fusion.4 = f32[1536]{0:T(1024)S(1)} fusion(f32[1536]{0:T(1024)S(1)} %copy-done.9, bf16[512,768]{1,0:T(8,128)(2,1)S(1)} %copy-done, bf16[768,1536]{1,0:T(8,128)(2,1)} %all-gather.3.cloned.1.call-done, bf16[512,1536]{1,0:T(8,128)(2,1)S(1)} %copy-done.1), kind=kOutput, calls=%fused_computation.9 | convolution fusion | flops 1211103744 | bytes 4730880 | tf_op jit(solution)/shard_map/dot_general | solution.py:53
  135.4 41.0 %all-reduce = (f32[1,1536]{1,0:T(1,128)S(1)}, f32[1536]{0:T(1024)S(1)}) all-reduce(f32[1,1536]{1,0:T(1,128)S(1)} %stack.28, f32[1536]{0:T(1024)S(1)} %convert_reduce_fusion), channel_id=1, replica_groups=mesh['dp'=8,'group'=4] {'dp','group'}, use_global_device_ids=true, to_apply=%region_5.0 | all-reduce | flops 3072 | bytes 24576 | tf_op jit(solution)/shard_map/psum | solution.py:57
  176.4 0.0 copy-done.6
  176.4 0.7 multiply_subtract_fusion.1
  177.1 0.0 all-gather.5.cloned.1.call-done
  177.1 2.8 %fusion.3 = bf16[128,1536]{0,1:T(8,128)(2,1)S(1)} fusion(bf16[768,1536]{1,0:T(8,128)(2,1)} %all-gather.5.cloned.1.call-done, bf16[128,768]{1,0:T(8,128)(2,1)S(1)} %copy-done.10, bf16[128,1536]{0,1:T(8,128)(2,1)S(1)} %copy.25, f32[1536]{0:T(1024)S(1)} %get-tuple-element.23, f32[1536]{0:T(1024)S(1)} %get-tuple-element.22), kind=kOutput, calls=%fused_computation.8 | convolution fusion | flops 302972928 | bytes 3354624 | tf_op jit(solution)/shard_map/dot_general | solution.py:73
  179.9 0.9 copy.26
  180.8 0.0 copy-done.5
  (19 shorter events, 0.1 us)
Async XLA Ops:
  7.2 1.1 copy-start
  7.2 44.6 %reduce-scatter.2.cloned.1.call-start = ((), (), s32[]{:S(2)}) async-start(), calls=%async_computation.1 | async-start | bytes 2654208 | tf_op jit(solution)/shard_map/reduce_scatter | solution.py:43
  12.5 84.7 %copy-start.2 = (f32[96,1536]{1,0:T(8,128)S(1)}, f32[96,1536]{1,0:T(8,128)}, u32[]{:S(2)}) copy-start(f32[96,1536]{1,0:T(8,128)} %param.16) | copy-start | bytes 1769476
  12.5 84.7 %copy-start.3 = (f32[96,1536]{1,0:T(8,128)S(1)}, f32[96,1536]{1,0:T(8,128)}, u32[]{:S(2)}) copy-start(f32[96,1536]{1,0:T(8,128)} %param.23) | copy-start | bytes 1769476
  12.6 84.7 %copy-start.4 = (f32[1536]{0:T(1024)S(1)}, f32[1536]{0:T(1024)}, u32[]{:S(2)}) copy-start(f32[1536]{0:T(1024)} %param.20) | copy-start | bytes 18436
  12.6 84.6 %all-reduce.3.cloned.1.call-start = ((), (), s32[]{:S(2)}) async-start(), calls=%async_computation.2 | async-start | bytes 589824 | tf_op jit(solution)/shard_map/psum | solution.py:58
  51.8 50.0 %copy-start.8 = (f32[1536]{0:T(1024)S(1)}, f32[1536]{0:T(1024)}, u32[]{:S(2)}) copy-start(f32[1536]{0:T(1024)} %param.24) | copy-start | bytes 18436
  51.8 51.9 %copy-start.1 = (bf16[512,1536]{1,0:T(8,128)(2,1)S(1)}, bf16[512,1536]{1,0:T(8,128)(2,1)}, u32[]{:S(2)}) copy-start(bf16[512,1536]{1,0:T(8,128)(2,1)} %param.15) | copy-start | bytes 4718596
  51.8 80.4 %all-gather.3.cloned.1.call-start = ((), (), s32[]{:S(2)}) async-start(), calls=%async_computation.3 | async-start | bytes 2654208 | tf_op jit(solution)/shard_map/all_gather | solution.py:54
  100.5 31.8 %copy-start.9 = (f32[1536]{0:T(1024)S(1)}, f32[1536]{0:T(1024)}, u32[]{:S(2)}) copy-start(f32[1536]{0:T(1024)} %param.19) | copy-start | bytes 18436
  100.5 76.6 %all-gather.5.cloned.1.call-start = ((), (), s32[]{:S(2)}) async-start(), calls=%async_computation.4 | async-start | bytes 2654208 | tf_op jit(solution)/shard_map/all_gather | solution.py:75
  104.0 72.3 %copy-start.6 = (f32[2,1536]{1,0:T(2,128)S(1)}, f32[2,1536]{1,0:T(2,128)}, u32[]{:S(2)}) copy-start(f32[2,1536]{1,0:T(2,128)} %param.21) | copy-start | bytes 36868
  104.0 72.3 %copy-start.7 = (f32[2,1536]{1,0:T(2,128)S(1)}, f32[2,1536]{1,0:T(2,128)}, u32[]{:S(2)}) copy-start(f32[2,1536]{1,0:T(2,128)} %param.22) | copy-start | bytes 36868
  104.0 73.1 %copy-start.10 = (bf16[128,768]{1,0:T(8,128)(2,1)S(1)}, bf16[128,768]{1,0:T(8,128)(2,1)}, u32[]{:S(2)}) copy-start(bf16[128,768]{1,0:T(8,128)(2,1)} %param.26) | copy-start | bytes 589828
  177.1 3.8 %copy-start.5 = (f32[2,1536]{1,0:T(2,128)}, f32[2,1536]{1,0:T(2,128)S(1)}, u32[]{:S(2)}) copy-start(f32[2,1536]{1,0:T(2,128)S(1)} %get-tuple-element.42) | copy-start | bytes 36868
Sparse Core Ops, SparseCore 0:
  12.7 39.0 reduce-scatter.1
  54.7 42.4 all-reduce.2
  100.6 31.6 all-gather.2
  134.4 31.6 all-gather.4
where the time goes:
time: 188 us; the launch traced here: 187 us
  waiting for transfers between devices  113 us (60%)
  blocking collectives  41 us (22%)
  between operations  13.9 us (7%)
  matrix products  10.1 us (5%)
  local copies, waits for them, and re-layouts  4.74 us (3%)
  other arithmetic  4.23 us (2%)
    psum x1, waiting for transfers between devices, local(): summed = lax.psum(shard_part, 'group').astype(jnp.float32)  45.3 us
    psum x1, blocking collectives, local(): bias_sum, scale_sum = lax.psum((bias_part, scale_part), ('dp', 'group'))  41 us
    reduce_scatter x1, waiting for transfers between devices, local(): lax.psum_scatter(lax.dot_general(inputs, cotangent, (((0,), (0,)), ((), (...  39.2 us
    all_gather x1, waiting for transfers between devices, local(): lax.all_gather(narrow, 'dp', axis=0, tiled=True)  28.2 us
    dot_general x1, matrix products, local(): lax.dot_general(inputs, cotangent, (((0,), (0,)), ((), ())), preferred_el...  4.23 us
  transfers between devices with their start and end apart: 4, of which 3 were waited for; matrix products, arithmetic and copies ran while one was open for 4% of the time, Pallas kernels for 0%

commit v1 on v0

v1 whole, which is shorter than its diff:
```python
import functools

import jax
import jax.numpy as jnp
from jax import lax
from jax.experimental import pallas as pl
from jax.experimental.pallas import tpu as pltpu
from jax.sharding import PartitionSpec as P

BETA_ONE = 0.9
BETA_TWO = 0.999
LEARN_RATE = 0.0004
WEIGHT_DECAY = 0.04
EPSILON = 1e-08
MOMENTUM = 0.994
CORRECT_ONE = 1.0 - 0.9**10
CORRECT_TWO = 1.0 - 0.999**10
PIECES = 4
F32 = jnp.float32
BF16 = jnp.bfloat16


def adam_update(param, first, second, grad, decay):
    first = BETA_ONE * first + (1.0 - BETA_ONE) * grad
    second = BETA_TWO * second + (1.0 - BETA_TWO) * grad * grad
    direction = first / CORRECT_ONE / (jnp.sqrt(second / CORRECT_TWO) + EPSILON) + decay * param
    return (param - LEARN_RATE * direction, first, second, direction)


def exchange(
    ndp,
    ngroup,
    att_hbm,
    cot_hbm,
    weight_hbm,
    tweight_hbm,
    tatt_hbm,
    tres_hbm,
    bias_ref,
    scale_ref,
    tbias_ref,
    tscale_ref,
    grad_ref,
    sums_ref,
    tout_ref,
    att,
    cot,
    weight,
    tweight,
    tatt,
    tres,
    tgather,
    part,
    from_core,
    acc,
    narrow,
    got_a,
    got_b,
    send_a,
    send_b,
    last_a,
    last_b,
    extra_out,
    extra_in,
    z_out,
    z_in,
    pieces,
    bias_slots,
    small_slots,
    load_sem,
    t_core_sem,
    t_up_sem,
    t_down_sem,
    t_recv,
    core_send,
    core_recv,
    plane_send,
    plane_recv,
    extra_send,
    extra_recv,
    z_send,
    z_recv,
    piece_send,
    piece_recv,
    bias_send,
    bias_recv,
    small_send,
    small_recv,
):
    line = ndp // 2
    half = line // 2
    i = lax.axis_index("dp")
    g = lax.axis_index("group")
    p = i // 2
    c = i % 2
    own = g % PIECES
    rows, width = weight.shape
    wide = width // PIECES

    def flip(index, bits):
        out = index
        bit = 1
        while bit <= bits:
            if bits & bit:
                out = out + bit - 2 * bit * ((index // bit) % 2)
            bit *= 2
        return out

    def remote(src, dst, send_sem, recv_sem, dp, group):
        return pltpu.make_async_remote_copy(
            src_ref=src,
            dst_ref=dst,
            send_sem=send_sem,
            recv_sem=recv_sem,
            device_id=(dp, group),
            device_id_type=pl.DeviceIdType.MESH,
        )

    loads = [
        pltpu.make_async_copy(src, dst, load_sem.at[k])
        for k, (src, dst) in enumerate(
            [
                (tweight_hbm, tweight),
                (weight_hbm, weight),
                (att_hbm, att),
                (cot_hbm, cot),
                (tatt_hbm, tatt),
                (tres_hbm, tres),
            ]
        )
    ]
    for load in loads:
        load.start()

    barrier = pltpu.get_barrier_semaphore()
    for k in range(1, ndp):
        pl.semaphore_signal(
            barrier, inc=1, device_id=(flip(i, k), g), device_id_type=pl.DeviceIdType.MESH
        )
    for k in range(1, ngroup):
        pl.semaphore_signal(
            barrier, inc=1, device_id=(i, flip(g, k)), device_id_type=pl.DeviceIdType.MESH
        )

    loads[0].wait()
    loads[1].wait()
    blended = MOMENTUM * tweight[...] + (1.0 - MOMENTUM) * weight[...]
    tgather[i] = blended.astype(BF16)
    pl.semaphore_wait(barrier, ndp - 1 + ngroup - 1)

    def t_copy(slot, send_sem, dp):
        return remote(tgather.at[slot], tgather.at[slot], send_sem, t_recv.at[slot], dp, g)

    mate = flip(i, 1)
    up = jnp.minimum(i + 2, ndp - 1)
    down = jnp.maximum(i - 2, 0)
    has_up = p < line - 1
    has_down = p > 0

    @pl.when(has_up)
    def _():
        t_copy(i, t_up_sem.at[0], i + 2).start()

    @pl.when(has_down)
    def _():
        t_copy(i, t_down_sem.at[0], i - 2).start()

    t_copy(i, t_core_sem.at[0], mate).start()

    def forward(d):
        @pl.when(p - d >= 0)
        def _():
            slot = i - 2 * d
            t_copy(slot, t_core_sem.at[2 * d - 1], mate).wait_recv()
            t_copy(slot, t_core_sem.at[2 * d - 1], mate).start()
            if d < line - 1:

                @pl.when(has_up)
                def _():
                    t_copy(slot, t_up_sem.at[d], i + 2).start()

        @pl.when(p + d < line)
        def _():
            slot = i + 2 * d
            t_copy(slot, t_core_sem.at[2 * d], mate).wait_recv()
            t_copy(slot, t_core_sem.at[2 * d], mate).start()
            if d < line - 1:

                @pl.when(has_down)
                def _():
                    t_copy(slot, t_down_sem.at[d], i - 2).start()

    loads[2].wait()
    turned = att[...].T
    loads[3].wait()
    order = [3, 1, 2, 0]
    core_copies = []
    for k in order:
        q = flip(own, k)
        columns = pl.ds(pl.multiple_of(q * wide, wide), wide)
        product = jnp.dot(turned, cot[:, columns], preferred_element_type=F32)
        product = product.reshape(line, 2, rows, wide).astype(BF16)
        part[0, q] = product[:, 0]
        part[1, q] = product[:, 1]
        copy = remote(
            part.at[1 - c, q], from_core.at[q], core_send.at[k], core_recv.at[k], mate, g
        )
        copy.start()
        core_copies.append(copy)

    ones = jnp.ones((8, cot.shape[0]), BF16)
    bias_slots[g] = jnp.dot(ones, cot[...], preferred_element_type=F32)
    bias_copies = [
        remote(
            bias_slots.at[g], bias_slots.at[g], bias_send.at[k], bias_recv.at[k], i, flip(g, k)
        )
        for k in range(1, ngroup)
    ]
    for copy in bias_copies:
        copy.start()

    x_mate = flip(g, 1)
    y_mate = flip(g, 2)
    low = pl.ds(0, half)
    high = pl.ds(half, half)

    def plane(n, src, dst, group):
        return remote(src, dst, plane_send.at[n], plane_recv.at[n], i, group)

    plane_copies = [
        plane(0, narrow.at[flip(own, 3), low], got_a.at[0], x_mate),
        plane(1, narrow.at[flip(own, 3), high], got_b.at[0], y_mate),
        plane(2, narrow.at[flip(own, 1), low], got_a.at[1], x_mate),
        plane(3, narrow.at[flip(own, 2), high], got_b.at[1], y_mate),
        plane(4, send_a, last_a, y_mate),
        plane(5, send_b, last_b, x_mate),
    ]
    after = {3: (0, 1), 1: (2,), 2: (3,), 0: ()}
    for n, k in enumerate(order):
        q = flip(own, k)
        core_copies[n].wait_recv()
        total = part[c, q].astype(F32) + from_core[q].astype(F32)
        acc[q] = total
        if k != 0:
            narrow[q] = total.astype(BF16)
        for m in after[k]:
            plane_copies[m].start()

    forward(1)

    plane_copies[0].wait_recv()
    send_a[...] = (acc[flip(own, 2), low] + got_a[0].astype(F32)).astype(BF16)
    plane_copies[4].start()
    plane_copies[1].wait_recv()
    send_b[...] = (acc[flip(own, 1), high] + got_b[0].astype(F32)).astype(BF16)
    plane_copies[5].start()
    plane_copies[2].wait_recv()
    acc[own, low] = acc[own, low] + got_a[1].astype(F32)
    plane_copies[3].wait_recv()
    acc[own, high] = acc[own, high] + got_b[1].astype(F32)

    for d in range(2, line - 1):
        forward(d)

    for copy in bias_copies:
        copy.wait_recv()
    bias_total = bias_slots[0, 0:1]
    for k in range(1, ngroup):
        bias_total = bias_total + bias_slots[k, 0:1]
    small_slots[i, 0:1] = bias_total

    plane_copies[4].wait_recv()
    acc[own, low] = acc[own, low] + last_a[...].astype(F32)
    plane_copies[5].wait_recv()
    acc[own, high] = acc[own, high] + last_b[...].astype(F32)

    extra_copies = []
    step = 0
    while PIECES << step < ngroup:
        extra_out[step] = acc[own].astype(BF16)
        copy = remote(
            extra_out.at[step],
            extra_in.at[step],
            extra_send.at[step],
            extra_recv.at[step],
            i,
            flip(g, PIECES << step),
        )
        copy.start()
        copy.wait_recv()
        acc[own] = extra_out[step].astype(F32) + extra_in[step].astype(F32)
        extra_copies.append(copy)
        step += 1

    z_out[...] = acc[own].astype(BF16)
    z_copies = []
    for k in range(line - 1, 0, -1):
        place = flip(p, k)
        copy = remote(
            z_out.at[place], z_in.at[k - 1], z_send.at[k - 1], z_recv.at[k - 1], 2 * place + c, g
        )
        copy.start()
        z_copies.append(copy)

    if line > 2:
        forward(line - 1)
    for k in range(line):
        slot = 2 * k + 1 - c
        t_copy(slot, t_core_sem.at[0], mate).wait_recv()
    if rows % 16 == 0:
        blended_all = tgather[...].reshape(ndp * rows, width)
    else:
        blended_all = tgather[...].astype(F32).reshape(ndp * rows, width).astype(BF16)
    loads[4].wait()
    loads[5].wait()
    branch = jnp.dot(tatt[...], blended_all, preferred_element_type=F32)
    new_bias = MOMENTUM * tbias_ref[...] + (1.0 - MOMENTUM) * bias_ref[...]
    new_scale = MOMENTUM * tscale_ref[...] + (1.0 - MOMENTUM) * scale_ref[...]
    tout_ref[...] = (tres[...].astype(F32) + new_scale * (branch + new_bias)).astype(BF16)

    total = acc[own, p]
    for copy in z_copies:
        copy.wait_recv()
    for k in range(line - 1):
        total = total + z_in[k].astype(F32)
    pieces[own] = total.astype(BF16)
    piece_copies = [
        remote(
            pieces.at[own],
            pieces.at[own],
            piece_send.at[k - 1],
            piece_recv.at[k - 1],
            i,
            flip(g, k),
        )
        for k in (3, 1, 2)
    ]
    for copy in piece_copies:
        copy.start()
    for copy in piece_copies:
        copy.wait_recv()
    for q in range(PIECES):
        columns = pl.ds(q * wide, wide)
        piece = pieces[q]
        grad_ref[:, columns] = piece
        rounded = weight[:, columns].astype(BF16).astype(F32)
        small_slots[i, 1:2, columns] = jnp.sum(rounded * piece.astype(F32), 0, keepdims=True)
    small_copies = [
        remote(
            small_slots.at[i],
            small_slots.at[i],
            small_send.at[k - 1],
            small_recv.at[k - 1],
            flip(i, k),
            g,
        )
        for k in range(1, ndp)
    ]
    for copy in small_copies:
        copy.start()
    for copy in small_copies:
        copy.wait_recv()
    sums = small_slots[0]
    for k in range(1, ndp):
        sums = sums + small_slots[k]
    sums_ref[0:1] = sums[0:1]
    sums_ref[1:2] = sums[1:2] + bias_ref[...] * sums[0:1]

    for copy in (
        core_copies + bias_copies + plane_copies + extra_copies + z_copies + piece_copies
    ):
        copy.wait_send()
    for copy in small_copies:
        copy.wait_send()
    t_copy(i, t_core_sem.at[0], mate).wait_send()

    @pl.when(has_up)
    def _():
        t_copy(i, t_up_sem.at[0], i + 2).wait_send()

    @pl.when(has_down)
    def _():
        t_copy(i, t_down_sem.at[0], i - 2).wait_send()

    for d in range(1, line):

        @pl.when(p - d >= 0)
        def _(d=d):
            slot = i - 2 * d
            t_copy(slot, t_core_sem.at[2 * d - 1], mate).wait_send()
            if d < line - 1:

                @pl.when(has_up)
                def _():
                    t_copy(slot, t_up_sem.at[d], i + 2).wait_send()

        @pl.when(p + d < line)
        def _(d=d):
            slot = i + 2 * d
            t_copy(slot, t_core_sem.at[2 * d], mate).wait_send()
            if d < line - 1:

                @pl.when(has_down)
                def _():
                    t_copy(slot, t_down_sem.at[d], i - 2).wait_send()


def local(
    ndp,
    ngroup,
    attended,
    cotangent,
    weight,
    weight_first,
    weight_second,
    bias,
    layer_scale,
    small_first,
    small_second,
    teacher_weight,
    teacher_bias,
    teacher_scale,
    teacher_attended,
    teacher_resid,
):
    total = attended.shape[0] * ndp * ngroup
    rows, width = weight.shape
    line = ndp // 2
    half = line // 2
    wide = width // PIECES
    extra = max(1, (ngroup // PIECES).bit_length() - 1)
    dma = pltpu.SemaphoreType.DMA
    anywhere = pl.BlockSpec(memory_space=pl.ANY)
    vmem = pl.BlockSpec(memory_space=pltpu.VMEM)
    summed, sums, teacher_out = pl.pallas_call(
        functools.partial(exchange, ndp, ngroup),
        out_shape=(
            jax.ShapeDtypeStruct((rows, width), BF16),
            jax.ShapeDtypeStruct((2, width), F32),
            jax.ShapeDtypeStruct(teacher_resid.shape, BF16),
        ),
        in_specs=[anywhere] * 6 + [vmem] * 4,
        out_specs=[vmem] * 3,
        scratch_shapes=[
            pltpu.VMEM(attended.shape, BF16),
            pltpu.VMEM(cotangent.shape, BF16),
            pltpu.VMEM((rows, width), F32),
            pltpu.VMEM((rows, width), F32),
            pltpu.VMEM(teacher_attended.shape, BF16),
            pltpu.VMEM(teacher_resid.shape, BF16),
            pltpu.VMEM((ndp, rows, width), BF16),
            pltpu.VMEM((2, PIECES, line, rows, wide), BF16),
            pltpu.VMEM((PIECES, line, rows, wide), BF16),
            pltpu.VMEM((PIECES, line, rows, wide), F32),
            pltpu.VMEM((PIECES, line, rows, wide), BF16),
            pltpu.VMEM((2, half, rows, wide), BF16),
            pltpu.VMEM((2, half, rows, wide), BF16),
            pltpu.VMEM((half, rows, wide), BF16),
            pltpu.VMEM((half, rows, wide), BF16),
            pltpu.VMEM((half, rows, wide), BF16),
            pltpu.VMEM((half, rows, wide), BF16),
            pltpu.VMEM((extra, line, rows, wide), BF16),
            pltpu.VMEM((extra, line, rows, wide), BF16),
            pltpu.VMEM((line, rows, wide), BF16),
            pltpu.VMEM((line - 1, rows, wide), BF16),
            pltpu.VMEM((PIECES, rows, wide), BF16),
            pltpu.VMEM((ngroup, 8, width), F32),
            pltpu.VMEM((ndp, 2, width), F32),
            dma((6,)),
            dma((2 * line,)),
            dma((line,)),
            dma((line,)),
            dma((ndp,)),
            dma((PIECES,)),
            dma((PIECES,)),
            dma((6,)),
            dma((6,)),
            dma((extra,)),
            dma((extra,)),
            dma((line - 1,)),
            dma((line - 1,)),
            dma((PIECES - 1,)),
            dma((PIECES - 1,)),
            dma((ngroup,)),
            dma((ngroup,)),
            dma((ndp - 1,)),
            dma((ndp - 1,)),
        ],
        compiler_params=pltpu.CompilerParams(
            collective_id=0, has_side_effects=True, vmem_limit_bytes=40 * 1024 * 1024
        ),
    )(
        attended,
        cotangent,
        weight,
        teacher_weight,
        teacher_attended,
        teacher_resid,
        bias[None, :],
        layer_scale[None, :],
        teacher_bias[None, :],
        teacher_scale[None, :],
    )
    grad_weight = summed.astype(F32) * layer_scale[None, :] / total
    grad_small = jnp.stack([layer_scale * sums[0], sums[1]]) / total
    new_weight, new_weight_first, new_weight_second, weight_direction = adam_update(
        weight, weight_first, weight_second, grad_weight, WEIGHT_DECAY
    )
    small = jnp.stack([bias, layer_scale])
    new_small, new_small_first, new_small_second, small_direction = adam_update(
        small, small_first, small_second, grad_small, 0.0
    )
    new_teacher_weight = MOMENTUM * teacher_weight + (1.0 - MOMENTUM) * weight
    new_teacher_small = (
        MOMENTUM * jnp.stack([teacher_bias, teacher_scale]) + (1.0 - MOMENTUM) * small
    )
    return (
        new_weight,
        new_weight_first,
        new_weight_second,
        weight_direction,
        new_teacher_weight,
        new_small,
        new_small_first,
        new_small_second,
        small_direction,
        new_teacher_small,
        teacher_out,
    )


def solution(mesh):
    placed = (
        P(("dp", "group"), None),
        P(("dp", "group"), None),
        P("dp", None),
        P("dp", None),
        P("dp", None),
        P(),
        P(),
        P(),
        P(),
        P("dp", None),
        P(),
        P(),
        P(("dp", "group"), None),
        P(("dp", "group"), None),
    )
    return jax.shard_map(
        functools.partial(local, mesh.shape["dp"], mesh.shape["group"]),
        mesh=mesh,
        in_specs=placed,
        out_specs=(
            P("dp", None),
            P("dp", None),
            P("dp", None),
            P("dp", None),
            P("dp", None),
            P(),
            P(),
            P(),
            P(),
            P(),
            P(("dp", "group"), None),
        ),
        check_vma=False,
    )
```

time: 188 us -> 59.8 us (0.32)
  waiting for transfers between devices: 113 us -> 0 us
  Pallas kernels: 0 us -> 45.7 us
  blocking collectives: 41 us -> 0 us
  between operations: 13.9 us -> 0.72 us
  matrix products: 10.1 us -> 0 us
  local copies, waits for them, and re-layouts: 4.74 us -> 10.2 us
    pallas_call x0 -> x1, Pallas kernels: none -> 45.7 us  [local(): pl.pallas_call(functools.partial(exchange, ndp, ngroup), out_shape=(jax.S...]
    psum x1 -> x0, waiting for transfers between devices: 45.3 us -> none  [local(): summed = lax.psum(shard_part, 'group').astype(jnp.float32)]
    psum x1 -> x0, blocking collectives: 41 us -> none  [local(): bias_sum, scale_sum = lax.psum((bias_part, scale_part), ('dp', 'group'))]
    reduce_scatter x1 -> x0, waiting for transfers between devices: 39.2 us -> none  [local(): lax.psum_scatter(lax.dot_general(inputs, cotangent, (((0,), (0,)), ((), (...]
    all_gather x2 -> x0, waiting for transfers between devices: 28.3 us -> none  [the longest x1 28.2 us: local(): lax.all_gather(narrow, 'dp', axis=0, tiled=True)]
    dot_general x3 -> x0, matrix products: 10.1 us -> none  [the longest x1 4.23 us: local(): lax.dot_general(inputs, cotangent, (((0,), (0,)), ((), ())), preferred_el...]
    unnamed x24 -> x23, local copies, waits for them, and re-layouts: 3.27 us -> 7.36 us
    convert_element_type x1 -> x0, other arithmetic: 3.27 us -> none  [local(): new_teacher_weight.astype(jnp.bfloat16)]
  transfers between devices with their start and end apart: 4 -> 0, of which waited for: 3 -> 0; matrix products, arithmetic and copies ran while one was open for 4% -> 0% of each run, Pallas kernels for 0% -> 0%
where the time goes in v1:
time: 59.8 us; the launch traced here: 59.3 us
  Pallas kernels  45.7 us (76%)
  local copies, waits for them, and re-layouts  10.2 us (17%)
  other arithmetic  2.62 us (4%)
  between operations  0.72 us (1%)
    pallas_call x1, Pallas kernels, local(): pl.pallas_call(functools.partial(exchange, ndp, ngroup), out_shape=(jax.S...  45.7 us
    unnamed x23, local copies, waits for them, and re-layouts  7.36 us
    sub x2, other arithmetic, adam_update(): return (param - LEARN_RATE * direction, first, second, direction)  2.62 us

profile of v1, /device:TPU:0, one launch (start us, length us, event | category | flops | bytes accessed | tf_op | source)
XLA Modules:
  0.0 59.3 jit_solution(4150693853938718963)
XLA Ops:
  0.6 0.7 %broadcast_in_dim.13.bias_ref = f32[1,1536]{1,0:T(1,128)S(1)} reshape(f32[1536]{0:T(1024)} %param.19) | data formatting | bytes 12288 | tf_op jit(solution)/shard_map/broadcast_in_dim | solution.py:499
  1.3 0.7 %broadcast_in_dim.15.tbias_ref = f32[1,1536]{1,0:T(1,128)S(1)} reshape(f32[1536]{0:T(1024)} %param.24) | data formatting | bytes 12288 | tf_op jit(solution)/shard_map/broadcast_in_dim | solution.py:501
  2.0 0.7 %broadcast_in_dim.16.tscale_ref = f32[1,1536]{1,0:T(1,128)S(1)} reshape(f32[1536]{0:T(1024)} %param.25) | data formatting | bytes 12288 | tf_op jit(solution)/shard_map/broadcast_in_dim | solution.py:502
  2.7 0.7 %broadcast_in_dim.14.scale_ref = f32[1,1536]{1,0:T(1,128)S(1)} reshape(f32[1536]{0:T(1024)} %param.20) | data formatting | bytes 12288 | tf_op jit(solution)/shard_map/broadcast_in_dim | solution.py:500
  3.5 0.0 copy-start
  3.5 1.1 %copy-done = f32[96,1536]{1,0:T(8,128)S(1)} copy-done((f32[96,1536]{1,0:T(8,128)S(1)}, f32[96,1536]{1,0:T(8,128)}, u32[]{:S(2)}) %copy-start) | copy-done | bytes 589848
  4.5 0.0 copy-start.1
  4.5 1.1 %copy-done.1 = f32[96,1536]{1,0:T(8,128)S(1)} copy-done((f32[96,1536]{1,0:T(8,128)S(1)}, f32[96,1536]{1,0:T(8,128)}, u32[]{:S(2)}) %copy-start.1) | copy-done | bytes 589848
  5.6 0.0 copy-start.2
  5.6 1.4 %copy-done.2 = bf16[512,1536]{1,0:T(8,128)(2,1)S(1)} copy-done((bf16[512,1536]{1,0:T(8,128)(2,1)S(1)}, bf16[512,1536]{1,0:T(8,128)(2,1)}, u32[]{:S(2)}) %copy-start.2) | copy-done | bytes 1572888
  7.0 0.0 copy-start.3
  7.0 1.1 %copy-done.3 = bf16[512,768]{1,0:T(8,128)(2,1)S(1)} copy-done((bf16[512,768]{1,0:T(8,128)(2,1)S(1)}, bf16[512,768]{1,0:T(8,128)(2,1)}, u32[]{:S(2)}) %copy-start.3) | copy-done | bytes 786456
  8.1 0.0 copy-start.4
  8.1 1.0 %copy-done.4 = bf16[128,1536]{1,0:T(8,128)(2,1)S(1)} copy-done((bf16[128,1536]{1,0:T(8,128)(2,1)S(1)}, bf16[128,1536]{1,0:T(8,128)(2,1)}, u32[]{:S(2)}) %copy-start.4) | copy-done | bytes 393240
  9.1 0.0 copy-start.5
  9.1 0.9 %copy-done.5 = bf16[128,768]{1,0:T(8,128)(2,1)S(1)} copy-done((bf16[128,768]{1,0:T(8,128)(2,1)S(1)}, bf16[128,768]{1,0:T(8,128)(2,1)}, u32[]{:S(2)}) %copy-start.5) | copy-done | bytes 196632
  10.0 0.0 copy-start.8
  10.0 0.0 copy-start.9
  10.0 0.0 copy-start.10
  10.1 0.0 copy-start.6
  10.1 0.0 copy-start.7
  10.1 45.7 %shard_map.221 = (bf16[96,1536]{1,0:T(8,128)(2,1)S(1)}, f32[2,1536]{1,0:T(2,128)S(1)}, bf16[128,1536]{1,0:T(8,128)(2,1)S(1)}) custom-call(bf16[512,768]{1,0:T(8,128)(2,1)S(1)} %copy-done.3, bf16[512,1536]{1,0:T(8,128)(2,1)S(1)} %copy-done.2, f32[96,1536]{1,0:T(8,128)S(1)} %copy-done, f32[96,1536]{1,0:T(8,128)S(1)} %copy-done.1, ...), custom_call_target="tpu_custom_call" | custom-call | tf_op jit(solution)/shard_map/pallas_call | solution.py:435
  55.8 0.0 copy-done.8
  55.9 0.0 copy-done.9
  55.9 0.0 copy-done.10
  55.9 0.7 %multiply_subtract_fusion.1 = (f32[2,1536]{1,0:T(2,128)}, f32[2,1536]{1,0:T(2,128)}, f32[2,1536]{1,0:T(2,128)}, f32[2,1536]{1,0:T(2,128)}, f32[2,1536]{1,0:T(2,128)}) fusion(f32[1,1536]{1,0:T(1,128)S(1)} %broadcast_in_dim.14.scale_ref, f32[1,1536]{1,0:T(1,128)S(1)} %broadcast_in_dim.13.bias_ref, f32[1,1536]{1,0:T(1,128)S(1)} %get-tuple-element.28, ...), kind=kLoop, calls=%fused_computation.10 | loop fusion | flops 67584 | bytes 122880 | tf_op jit(solution)/shard_map/sub | solution.py:27
  56.6 0.0 copy-done.6
  56.6 0.0 copy-done.7
  56.6 1.9 %multiply_subtract_fusion = (f32[96,1536]{1,0:T(8,128)}, f32[96,1536]{1,0:T(8,128)}, f32[96,1536]{1,0:T(8,128)}, f32[96,1536]{1,0:T(8,128)}, f32[96,1536]{1,0:T(8,128)}) fusion(f32[96,1536]{1,0:T(8,128)S(1)} %copy-done, f32[1536]{0:T(1024)S(1)} %copy-done.8, bf16[96,1536]{1,0:T(8,128)(2,1)S(1)} %get-tuple-element.14, f32[96,1536]{1,0:T(8,128)S(1)} %copy-done.6, ...), kind=kLoop, calls=%fused_computation.1 | loop fusion | flops 3096576 | bytes 5609472 | tf_op jit(solution)/shard_map/sub | solution.py:27
  58.5 0.7 %copy.26 = bf16[128,1536]{1,0:T(8,128)(2,1)} copy(bf16[128,1536]{1,0:T(8,128)(2,1)S(1)} %get-tuple-element.50) | data formatting | bytes 786432
  (3 shorter events, 0.0 us)
Async XLA Ops:
  3.5 1.1 %copy-start = (f32[96,1536]{1,0:T(8,128)S(1)}, f32[96,1536]{1,0:T(8,128)}, u32[]{:S(2)}) copy-start(f32[96,1536]{1,0:T(8,128)} %weight_hbm.1) | copy-start | bytes 1769476
  4.5 1.1 %copy-start.1 = (f32[96,1536]{1,0:T(8,128)S(1)}, f32[96,1536]{1,0:T(8,128)}, u32[]{:S(2)}) copy-start(f32[96,1536]{1,0:T(8,128)} %tweight_hbm.1) | copy-start | bytes 1769476
  5.6 1.4 %copy-start.2 = (bf16[512,1536]{1,0:T(8,128)(2,1)S(1)}, bf16[512,1536]{1,0:T(8,128)(2,1)}, u32[]{:S(2)}) copy-start(bf16[512,1536]{1,0:T(8,128)(2,1)} %cot_hbm.1) | copy-start | bytes 4718596
  7.0 1.1 %copy-start.3 = (bf16[512,768]{1,0:T(8,128)(2,1)S(1)}, bf16[512,768]{1,0:T(8,128)(2,1)}, u32[]{:S(2)}) copy-start(bf16[512,768]{1,0:T(8,128)(2,1)} %att_hbm.1) | copy-start | bytes 2359300
  8.1 1.0 %copy-start.4 = (bf16[128,1536]{1,0:T(8,128)(2,1)S(1)}, bf16[128,1536]{1,0:T(8,128)(2,1)}, u32[]{:S(2)}) copy-start(bf16[128,1536]{1,0:T(8,128)(2,1)} %tres_hbm.1) | copy-start | bytes 1179652
  9.1 0.9 %copy-start.5 = (bf16[128,768]{1,0:T(8,128)(2,1)S(1)}, bf16[128,768]{1,0:T(8,128)(2,1)}, u32[]{:S(2)}) copy-start(bf16[128,768]{1,0:T(8,128)(2,1)} %tatt_hbm.1) | copy-start | bytes 589828
  10.0 45.8 %copy-start.8 = (f32[1536]{0:T(1024)S(1)}, f32[1536]{0:T(1024)}, u32[]{:S(2)}) copy-start(f32[1536]{0:T(1024)} %param.20) | copy-start | bytes 18436
  10.0 45.8 %copy-start.9 = (f32[2,1536]{1,0:T(2,128)S(1)}, f32[2,1536]{1,0:T(2,128)}, u32[]{:S(2)}) copy-start(f32[2,1536]{1,0:T(2,128)} %param.21) | copy-start | bytes 36868
  10.0 45.8 %copy-start.10 = (f32[2,1536]{1,0:T(2,128)S(1)}, f32[2,1536]{1,0:T(2,128)}, u32[]{:S(2)}) copy-start(f32[2,1536]{1,0:T(2,128)} %param.22) | copy-start | bytes 36868
  10.1 46.5 %copy-start.6 = (f32[96,1536]{1,0:T(8,128)S(1)}, f32[96,1536]{1,0:T(8,128)}, u32[]{:S(2)}) copy-start(f32[96,1536]{1,0:T(8,128)} %param.17) | copy-start | bytes 1769476
  10.1 46.5 %copy-start.7 = (f32[96,1536]{1,0:T(8,128)S(1)}, f32[96,1536]{1,0:T(8,128)}, u32[]{:S(2)}) copy-start(f32[96,1536]{1,0:T(8,128)} %param.18) | copy-start | bytes 1769476

commit v2 on v1

--- a/solution.py
+++ b/solution.py
@@ -27,28 +27,90 @@
     return (param - LEARN_RATE * direction, first, second, direction)
 
 
+def finish(
+    total,
+    grad_ref,
+    sums_ref,
+    branch_ref,
+    weight_ref,
+    first_ref,
+    second_ref,
+    bias_ref,
+    scale_ref,
+    small_first_ref,
+    small_second_ref,
+    tweight_ref,
+    tbias_ref,
+    tscale_ref,
+    tres_ref,
+    *rest,
+):
+    outs, held, sem = rest[:11], rest[11:22], rest[22]
+    rows, width = weight_ref.shape
+    chunk = rows // 3 if rows % 24 == 0 else rows
+    chunks = rows // chunk
+    copies = []
+
+    def send(n, where=None, k=0):
+        src, dst = held[n], outs[n]
+        if where is not None:
+            src, dst = src.at[where], dst.at[where]
+        copy = pltpu.make_async_copy(src, dst, sem.at[n, k])
+        copy.start()
+        copies.append(copy)
+
+    scale = scale_ref[...][None, :]
+    for k in range(chunks):
+        where = pl.ds(k * chunk, chunk)
+        grad = grad_ref[where] * scale / total
+        param = weight_ref[where]
+        held[4][where] = MOMENTUM * tweight_ref[where] + (1.0 - MOMENTUM) * param
+        results = adam_update(param, first_ref[where], second_ref[where], grad, WEIGHT_DECAY)
+        for n, result in enumerate(results):
+            held[n][where] = result
+        for n in range(5):
+            send(n, where, k)
+    bias = bias_ref[...][None, :]
+    small = (bias, scale)
+    bias_sum = sums_ref[0:1]
+    scale_sum = sums_ref[1:2] + bias * bias_sum
+    small_grad = (scale * bias_sum / total, scale_sum / total)
+    blended = []
+    for r, old in enumerate((tbias_ref, tscale_ref)):
+        row = pl.ds(r, 1)
+        results = adam_update(
+            small[r], small_first_ref[row], small_second_ref[row], small_grad[r], 0.0
+        )
+        blended.append(MOMENTUM * old[...][None, :] + (1.0 - MOMENTUM) * small[r])
+        for n, result in enumerate((*results, blended[r])):
+            held[5 + n][row] = result
+    for n in range(5, 10):
+        send(n)
+    held[10][...] = (
+        tres_ref[...].astype(F32) + blended[1] * (branch_ref[...] + blended[0])
+    ).astype(BF16)
+    send(10)
+    for copy in copies:
+        copy.wait()
+
+
 def exchange(
     ndp,
     ngroup,
+    weight_hbm,
+    tweight_hbm,
     att_hbm,
     cot_hbm,
-    weight_hbm,
-    tweight_hbm,
     tatt_hbm,
-    tres_hbm,
-    bias_ref,
-    scale_ref,
-    tbias_ref,
-    tscale_ref,
     grad_ref,
     sums_ref,
-    tout_ref,
+    branch_ref,
+    weight,
+    tweight,
     att,
     cot,
-    weight,
-    tweight,
     tatt,
-    tres,
+    load_sem,
     tgather,
     part,
     from_core,
@@ -66,8 +128,9 @@
     z_in,
     pieces,
     bias_slots,
-    small_slots,
-    load_sem,
+    bias_all,
+    scale_slots,
+    scale_pieces,
     t_core_sem,
     t_up_sem,
     t_down_sem,
@@ -84,8 +147,12 @@
     piece_recv,
     bias_send,
     bias_recv,
-    small_send,
-    small_recv,
+    bias_all_send,
+    bias_all_recv,
+    scale_send,
+    scale_recv,
+    scale_piece_send,
+    scale_piece_recv,
 ):
     line = ndp // 2
     half = line // 2
@@ -120,12 +187,11 @@
         pltpu.make_async_copy(src, dst, load_sem.at[k])
         for k, (src, dst) in enumerate(
             [
+                (weight_hbm, weight),
                 (tweight_hbm, tweight),
-                (weight_hbm, weight),
                 (att_hbm, att),
                 (cot_hbm, cot),
                 (tatt_hbm, tatt),
-                (tres_hbm, tres),
             ]
         )
     ]
@@ -144,8 +210,7 @@
 
     loads[0].wait()
     loads[1].wait()
-    blended = MOMENTUM * tweight[...] + (1.0 - MOMENTUM) * weight[...]
-    tgather[i] = blended.astype(BF16)
+    tgather[i] = (MOMENTUM * tweight[...] + (1.0 - MOMENTUM) * weight[...]).astype(BF16)
     pl.semaphore_wait(barrier, ndp - 1 + ngroup - 1)
 
     def t_copy(slot, send_sem, dp):
@@ -193,6 +258,7 @@
     loads[2].wait()
     turned = att[...].T
     loads[3].wait()
+
     order = [3, 1, 2, 0]
     core_copies = []
     for k in order:
@@ -267,7 +333,20 @@
     bias_total = bias_slots[0, 0:1]
     for k in range(1, ngroup):
         bias_total = bias_total + bias_slots[k, 0:1]
-    small_slots[i, 0:1] = bias_total
+    bias_all[i] = bias_total
+    bias_all_copies = [
+        remote(
+            bias_all.at[i],
+            bias_all.at[i],
+            bias_all_send.at[k - 1],
+            bias_all_recv.at[k - 1],
+            flip(i, k),
+            g,
+        )
+        for k in range(1, ndp)
+    ]
+    for copy in bias_all_copies:
+        copy.start()
 
     plane_copies[4].wait_recv()
     acc[own, low] = acc[own, low] + last_a[...].astype(F32)
@@ -312,11 +391,7 @@
     else:
         blended_all = tgather[...].astype(F32).reshape(ndp * rows, width).astype(BF16)
     loads[4].wait()
-    loads[5].wait()
-    branch = jnp.dot(tatt[...], blended_all, preferred_element_type=F32)
-    new_bias = MOMENTUM * tbias_ref[...] + (1.0 - MOMENTUM) * bias_ref[...]
-    new_scale = MOMENTUM * tscale_ref[...] + (1.0 - MOMENTUM) * scale_ref[...]
-    tout_ref[...] = (tres[...].astype(F32) + new_scale * (branch + new_bias)).astype(BF16)
+    branch_ref[...] = jnp.dot(tatt[...], blended_all, preferred_element_type=F32)
 
     total = acc[own, p]
     for copy in z_copies:
@@ -337,40 +412,61 @@
     ]
     for copy in piece_copies:
         copy.start()
+    columns = pl.ds(pl.multiple_of(own * wide, wide), wide)
+    rounded = weight[:, columns].astype(BF16).astype(F32)
+    scale_slots[i] = jnp.sum(rounded * pieces[own].astype(F32), 0, keepdims=True)
+    scale_copies = [
+        remote(
+            scale_slots.at[i],
+            scale_slots.at[i],
+            scale_send.at[k - 1],
+            scale_recv.at[k - 1],
+            flip(i, k),
+            g,
+        )
+        for k in range(ndp - 1, 0, -1)
+    ]
+    for copy in scale_copies:
+        copy.start()
+    for copy in bias_all_copies:
+        copy.wait_recv()
+    bias_sum = bias_all[0]
+    for k in range(1, ndp):
+        bias_sum = bias_sum + bias_all[k]
+    sums_ref[0:1] = bias_sum
+    for copy in scale_copies:
+        copy.wait_recv()
+    scale_sum = scale_slots[0]
+    for k in range(1, ndp):
+        scale_sum = scale_sum + scale_slots[k]
+    scale_pieces[own] = scale_sum
+    scale_piece_copies = [
+        remote(
+            scale_pieces.at[own],
+            scale_pieces.at[own],
+            scale_piece_send.at[k - 1],
+            scale_piece_recv.at[k - 1],
+            i,
+            flip(g, k),
+        )
+        for k in (3, 1, 2)
+    ]
+    for copy in scale_piece_copies:
+        copy.start()
     for copy in piece_copies:
         copy.wait_recv()
     for q in range(PIECES):
-        columns = pl.ds(q * wide, wide)
-        piece = pieces[q]
-        grad_ref[:, columns] = piece
-        rounded = weight[:, columns].astype(BF16).astype(F32)
-        small_slots[i, 1:2, columns] = jnp.sum(rounded * piece.astype(F32), 0, keepdims=True)
-    small_copies = [
-        remote(
-            small_slots.at[i],
-            small_slots.at[i],
-            small_send.at[k - 1],
-            small_recv.at[k - 1],
-            flip(i, k),
-            g,
-        )
-        for k in range(1, ndp)
-    ]
-    for copy in small_copies:
-        copy.start()
-    for copy in small_copies:
+        grad_ref[:, pl.ds(q * wide, wide)] = pieces[q].astype(F32)
+    for copy in scale_piece_copies:
         copy.wait_recv()
-    sums = small_slots[0]
-    for k in range(1, ndp):
-        sums = sums + small_slots[k]
-    sums_ref[0:1] = sums[0:1]
-    sums_ref[1:2] = sums[1:2] + bias_ref[...] * sums[0:1]
+    for q in range(PIECES):
+        sums_ref[1:2, pl.ds(q * wide, wide)] = scale_pieces[q]
 
     for copy in (
         core_copies + bias_copies + plane_copies + extra_copies + z_copies + piece_copies
     ):
         copy.wait_send()
-    for copy in small_copies:
+    for copy in bias_all_copies + scale_copies + scale_piece_copies:
         copy.wait_send()
     t_copy(i, t_core_sem.at[0], mate).wait_send()
 
@@ -430,24 +526,29 @@
     wide = width // PIECES
     extra = max(1, (ngroup // PIECES).bit_length() - 1)
     dma = pltpu.SemaphoreType.DMA
-    anywhere = pl.BlockSpec(memory_space=pl.ANY)
+    hbm = pl.BlockSpec(memory_space=pltpu.HBM)
     vmem = pl.BlockSpec(memory_space=pltpu.VMEM)
-    summed, sums, teacher_out = pl.pallas_call(
+    limit = 60 * 1024 * 1024
+
+    def like(array, dtype=None):
+        return jax.ShapeDtypeStruct(array.shape, dtype or array.dtype)
+
+    summed, sums, branch = pl.pallas_call(
         functools.partial(exchange, ndp, ngroup),
         out_shape=(
-            jax.ShapeDtypeStruct((rows, width), BF16),
+            jax.ShapeDtypeStruct((rows, width), F32),
             jax.ShapeDtypeStruct((2, width), F32),
-            jax.ShapeDtypeStruct(teacher_resid.shape, BF16),
+            like(teacher_resid, F32),
         ),
-        in_specs=[anywhere] * 6 + [vmem] * 4,
+        in_specs=[hbm] * 5,
         out_specs=[vmem] * 3,
         scratch_shapes=[
+            pltpu.VMEM((rows, width), F32),
+            pltpu.VMEM((rows, width), F32),
             pltpu.VMEM(attended.shape, BF16),
             pltpu.VMEM(cotangent.shape, BF16),
-            pltpu.VMEM((rows, width), F32),
-            pltpu.VMEM((rows, width), F32),
             pltpu.VMEM(teacher_attended.shape, BF16),
-            pltpu.VMEM(teacher_resid.shape, BF16),
+            dma((5,)),
             pltpu.VMEM((ndp, rows, width), BF16),
             pltpu.VMEM((2, PIECES, line, rows, wide), BF16),
             pltpu.VMEM((PIECES, line, rows, wide), BF16),
@@ -465,8 +566,9 @@
             pltpu.VMEM((line - 1, rows, wide), BF16),
             pltpu.VMEM((PIECES, rows, wide), BF16),
             pltpu.VMEM((ngroup, 8, width), F32),
-            pltpu.VMEM((ndp, 2, width), F32),
-            dma((6,)),
+            pltpu.VMEM((ndp, 1, width), F32),
+            pltpu.VMEM((ndp, 1, wide), F32),
+            pltpu.VMEM((PIECES, 1, wide), F32),
             dma((2 * line,)),
             dma((line,)),
             dma((line,)),
@@ -485,47 +587,40 @@
             dma((ngroup,)),
             dma((ndp - 1,)),
             dma((ndp - 1,)),
+            dma((ndp - 1,)),
+            dma((ndp - 1,)),
+            dma((PIECES - 1,)),
+            dma((PIECES - 1,)),
         ],
         compiler_params=pltpu.CompilerParams(
-            collective_id=0, has_side_effects=True, vmem_limit_bytes=40 * 1024 * 1024
+            collective_id=0, has_side_effects=True, vmem_limit_bytes=limit
         ),
+    )(weight, teacher_weight, attended, cotangent, teacher_attended)
+    large = [like(weight)] * 5
+    little = [like(small_first)] * 5
+    out_shape = (*large, *little, like(teacher_resid))
+    return pl.pallas_call(
+        functools.partial(finish, total),
+        out_shape=out_shape,
+        in_specs=[vmem] * 14,
+        out_specs=[hbm] * 11,
+        scratch_shapes=[pltpu.VMEM(o.shape, o.dtype) for o in out_shape] + [dma((11, 3))],
+        compiler_params=pltpu.CompilerParams(vmem_limit_bytes=limit),
     )(
-        attended,
-        cotangent,
+        summed,
+        sums,
+        branch,
         weight,
+        weight_first,
+        weight_second,
+        bias,
+        layer_scale,
+        small_first,
+        small_second,
         teacher_weight,
-        teacher_attended,
+        teacher_bias,
+        teacher_scale,
         teacher_resid,
-        bias[None, :],
-        layer_scale[None, :],
-        teacher_bias[None, :],
-        teacher_scale[None, :],
-    )
-    grad_weight = summed.astype(F32) * layer_scale[None, :] / total
-    grad_small = jnp.stack([layer_scale * sums[0], sums[1]]) / total
-    new_weight, new_weight_first, new_weight_second, weight_direction = adam_update(
-        weight, weight_first, weight_second, grad_weight, WEIGHT_DECAY
-    )
-    small = jnp.stack([bias, layer_scale])
-    new_small, new_small_first, new_small_second, small_direction = adam_update(
-        small, small_first, small_second, grad_small, 0.0
-    )
-    new_teacher_weight = MOMENTUM * teacher_weight + (1.0 - MOMENTUM) * weight
-    new_teacher_small = (
-        MOMENTUM * jnp.stack([teacher_bias, teacher_scale]) + (1.0 - MOMENTUM) * small
-    )
-    return (
-        new_weight,
-        new_weight_first,
-        new_weight_second,
-        weight_direction,
-        new_teacher_weight,
-        new_small,
-        new_small_first,
-        new_small_second,
-        small_direction,
-        new_teacher_small,
-        teacher_out,
     )
 
 

time: 59.8 us -> 49.7 us (0.83)
  local copies, waits for them, and re-layouts: 10.2 us -> 0 us
  Pallas kernels: 45.7 us -> 48.9 us
  other arithmetic: 2.62 us -> 0 us
    unnamed x23 -> x0, local copies, waits for them, and re-layouts: 7.36 us -> none
    pallas_call x0 -> x1, Pallas kernels: none -> 4.43 us  [local(): pl.pallas_call(functools.partial(finish, total), out_shape=out_shape, in_...]
    broadcast_in_dim x4 -> x0, local copies, waits for them, and re-layouts: 2.81 us -> none  [the longest x1 0.7 us: local(): bias[None, :]]
    sub x2 -> x0, other arithmetic: 2.62 us -> none  [adam_update(): return (param - LEARN_RATE * direction, first, second, direction)]
    pallas_call x1, Pallas kernels: 45.7 us -> 44.5 us  [local(): pl.pallas_call(functools.partial(exchange, ndp, ngroup), out_shape=(jax.S...]
where the time goes in v2:
time: 49.7 us; the launch traced here: 49.5 us
  Pallas kernels  48.9 us (98%)
  between operations  0.65 us (1%)
    pallas_call x1, Pallas kernels, local(): pl.pallas_call(functools.partial(exchange, ndp, ngroup), out_shape=(jax.S...  44.5 us
    pallas_call x1, Pallas kernels, local(): pl.pallas_call(functools.partial(finish, total), out_shape=out_shape, in_...  4.43 us

profile of v2, /device:TPU:0, one launch (start us, length us, event | category | flops | bytes accessed | tf_op | source)
XLA Modules:
  0.0 49.5 jit_solution(12312171692426574432)
XLA Ops:
  0.6 44.5 %shard_map.221 = (f32[96,1536]{1,0:T(8,128)}, f32[2,1536]{1,0:T(2,128)}, f32[128,1536]{1,0:T(8,128)}) custom-call(f32[96,1536]{1,0:T(8,128)} %weight_ref.1, f32[96,1536]{1,0:T(8,128)} %tweight_ref.1, bf16[512,768]{1,0:T(8,128)(2,1)} %att_hbm.1, bf16[512,1536]{1,0:T(8,128)(2,1)} %cot_hbm.1, bf16[128,768]{1,0:T(8,128)(2,1)} %tatt_hbm.1), custom_call_target="tpu_custom_call" | custom-call | tf_op jit(solution)/shard_map/pallas_call | solution.py:536
  45.1 4.4 %shard_map.222 = (f32[96,1536]{1,0:T(8,128)}, f32[96,1536]{1,0:T(8,128)}, f32[96,1536]{1,0:T(8,128)}, f32[96,1536]{1,0:T(8,128)}, f32[96,1536]{1,0:T(8,128)}, /*...) custom-call(f32[96,1536]{1,0:T(8,128)} %get-tuple-element.14.grad_re, ...), custom_call_target="tpu_custom_call" | custom-call | tf_op jit(solution)/shard_map/pallas_call | solution.py:602

commit v3 on v2

--- a/solution.py
+++ b/solution.py
@@ -287,21 +287,24 @@
 
     x_mate = flip(g, 1)
     y_mate = flip(g, 2)
-    low = pl.ds(0, half)
-    high = pl.ds(half, half)
+    quarter = half // 2
+    low = [pl.ds(h * quarter, quarter) for h in range(2)]
+    high = [pl.ds(half + h * quarter, quarter) for h in range(2)]
 
     def plane(n, src, dst, group):
         return remote(src, dst, plane_send.at[n], plane_recv.at[n], i, group)
 
-    plane_copies = [
-        plane(0, narrow.at[flip(own, 3), low], got_a.at[0], x_mate),
-        plane(1, narrow.at[flip(own, 3), high], got_b.at[0], y_mate),
-        plane(2, narrow.at[flip(own, 1), low], got_a.at[1], x_mate),
-        plane(3, narrow.at[flip(own, 2), high], got_b.at[1], y_mate),
-        plane(4, send_a, last_a, y_mate),
-        plane(5, send_b, last_b, x_mate),
-    ]
-    after = {3: (0, 1), 1: (2,), 2: (3,), 0: ()}
+    plane_copies = []
+    for h in range(2):
+        plane_copies += [
+            plane(6 * h, narrow.at[flip(own, 3), low[h]], got_a.at[h, 0], x_mate),
+            plane(6 * h + 1, narrow.at[flip(own, 3), high[h]], got_b.at[h, 0], y_mate),
+            plane(6 * h + 2, narrow.at[flip(own, 1), low[h]], got_a.at[h, 1], x_mate),
+            plane(6 * h + 3, narrow.at[flip(own, 2), high[h]], got_b.at[h, 1], y_mate),
+            plane(6 * h + 4, send_a.at[h], last_a.at[h], y_mate),
+            plane(6 * h + 5, send_b.at[h], last_b.at[h], x_mate),
+        ]
+    after = {3: (0, 1), 1: (2,), 2: (3,), 0: (6, 7, 8, 9)}
     for n, k in enumerate(order):
         q = flip(own, k)
         core_copies[n].wait_recv()
@@ -311,22 +314,6 @@
             narrow[q] = total.astype(BF16)
         for m in after[k]:
             plane_copies[m].start()
-
-    forward(1)
-
-    plane_copies[0].wait_recv()
-    send_a[...] = (acc[flip(own, 2), low] + got_a[0].astype(F32)).astype(BF16)
-    plane_copies[4].start()
-    plane_copies[1].wait_recv()
-    send_b[...] = (acc[flip(own, 1), high] + got_b[0].astype(F32)).astype(BF16)
-    plane_copies[5].start()
-    plane_copies[2].wait_recv()
-    acc[own, low] = acc[own, low] + got_a[1].astype(F32)
-    plane_copies[3].wait_recv()
-    acc[own, high] = acc[own, high] + got_b[1].astype(F32)
-
-    for d in range(2, line - 1):
-        forward(d)
 
     for copy in bias_copies:
         copy.wait_recv()
@@ -348,10 +335,44 @@
     for copy in bias_all_copies:
         copy.start()
 
-    plane_copies[4].wait_recv()
-    acc[own, low] = acc[own, low] + last_a[...].astype(F32)
-    plane_copies[5].wait_recv()
-    acc[own, high] = acc[own, high] + last_b[...].astype(F32)
+    def second(h):
+        plane_copies[6 * h].wait_recv()
+        send_a[h] = (acc[flip(own, 2), low[h]] + got_a[h, 0].astype(F32)).astype(BF16)
+        plane_copies[6 * h + 4].start()
+        plane_copies[6 * h + 1].wait_recv()
+        send_b[h] = (acc[flip(own, 1), high[h]] + got_b[h, 0].astype(F32)).astype(BF16)
+        plane_copies[6 * h + 5].start()
+
+    def third(h):
+        plane_copies[6 * h + 2].wait_recv()
+        plane_copies[6 * h + 4].wait_recv()
+        acc[own, low[h]] = acc[own, low[h]] + (got_a[h, 1].astype(F32) + last_a[h].astype(F32))
+        plane_copies[6 * h + 3].wait_recv()
+        plane_copies[6 * h + 5].wait_recv()
+        acc[own, high[h]] = acc[own, high[h]] + (got_b[h, 1].astype(F32) + last_b[h].astype(F32))
+
+    def z_copy(place, k):
+        return remote(
+            z_out.at[place], z_in.at[k - 1], z_send.at[k - 1], z_recv.at[k - 1], 2 * place + c, g
+        )
+
+    def to_line(h):
+        for first in (h * quarter, half + h * quarter):
+            where = pl.ds(first, quarter)
+            z_out[where] = acc[own, where].astype(BF16)
+            for place in range(first, first + quarter):
+
+                @pl.when(p != place)
+                def _(place=place):
+                    z_copy(place, flip(p, place)).start()
+
+    second(0)
+    forward(1)
+    second(1)
+    third(0)
+    if ngroup == PIECES:
+        to_line(0)
+    third(1)
 
     extra_copies = []
     step = 0
@@ -371,27 +392,12 @@
         extra_copies.append(copy)
         step += 1
 
-    z_out[...] = acc[own].astype(BF16)
-    z_copies = []
-    for k in range(line - 1, 0, -1):
-        place = flip(p, k)
-        copy = remote(
-            z_out.at[place], z_in.at[k - 1], z_send.at[k - 1], z_recv.at[k - 1], 2 * place + c, g
-        )
-        copy.start()
-        z_copies.append(copy)
-
-    if line > 2:
-        forward(line - 1)
-    for k in range(line):
-        slot = 2 * k + 1 - c
-        t_copy(slot, t_core_sem.at[0], mate).wait_recv()
-    if rows % 16 == 0:
-        blended_all = tgather[...].reshape(ndp * rows, width)
-    else:
-        blended_all = tgather[...].astype(F32).reshape(ndp * rows, width).astype(BF16)
-    loads[4].wait()
-    branch_ref[...] = jnp.dot(tatt[...], blended_all, preferred_element_type=F32)
+    if ngroup != PIECES:
+        to_line(0)
+    to_line(1)
+    for d in range(2, line - 1):
+        forward(d)
+    z_copies = [z_copy(flip(p, k), k) for k in range(1, line)]
 
     total = acc[own, p]
     for copy in z_copies:
@@ -428,6 +434,18 @@
     ]
     for copy in scale_copies:
         copy.start()
+    if line > 2:
+        forward(line - 1)
+    for k in range(line):
+        slot = 2 * k + 1 - c
+        t_copy(slot, t_core_sem.at[0], mate).wait_recv()
+    if rows % 16 == 0:
+        blended_all = tgather[...].reshape(ndp * rows, width)
+    else:
+        blended_all = tgather[...].astype(F32).reshape(ndp * rows, width).astype(BF16)
+    loads[4].wait()
+    branch_ref[...] = jnp.dot(tatt[...], blended_all, preferred_element_type=F32)
+
     for copy in bias_all_copies:
         copy.wait_recv()
     bias_sum = bias_all[0]
@@ -554,12 +572,12 @@
             pltpu.VMEM((PIECES, line, rows, wide), BF16),
             pltpu.VMEM((PIECES, line, rows, wide), F32),
             pltpu.VMEM((PIECES, line, rows, wide), BF16),
-            pltpu.VMEM((2, half, rows, wide), BF16),
-            pltpu.VMEM((2, half, rows, wide), BF16),
-            pltpu.VMEM((half, rows, wide), BF16),
-            pltpu.VMEM((half, rows, wide), BF16),
-            pltpu.VMEM((half, rows, wide), BF16),
-            pltpu.VMEM((half, rows, wide), BF16),
+            pltpu.VMEM((2, 2, half // 2, rows, wide), BF16),
+            pltpu.VMEM((2, 2, half // 2, rows, wide), BF16),
+            pltpu.VMEM((2, half // 2, rows, wide), BF16),
+            pltpu.VMEM((2, half // 2, rows, wide), BF16),
+            pltpu.VMEM((2, half // 2, rows, wide), BF16),
+            pltpu.VMEM((2, half // 2, rows, wide), BF16),
             pltpu.VMEM((extra, line, rows, wide), BF16),
             pltpu.VMEM((extra, line, rows, wide), BF16),
             pltpu.VMEM((line, rows, wide), BF16),
@@ -575,8 +593,8 @@
             dma((ndp,)),
             dma((PIECES,)),
             dma((PIECES,)),
-            dma((6,)),
-            dma((6,)),
+            dma((12,)),
+            dma((12,)),
             dma((extra,)),
             dma((extra,)),
             dma((line - 1,)),

time: 49.7 us -> 45.3 us (0.911)
  Pallas kernels: 48.9 us -> 44.5 us
    pallas_call x1, Pallas kernels: 44.5 us -> 40 us  [local(): pl.pallas_call(functools.partial(exchange, ndp, ngroup), out_shape=(jax.S...]
where the time goes in v3:
time: 45.3 us; the launch traced here: 45.1 us
  Pallas kernels  44.5 us (98%)
  between operations  0.65 us (1%)
    pallas_call x1, Pallas kernels, local(): pl.pallas_call(functools.partial(exchange, ndp, ngroup), out_shape=(jax.S...  40 us
    pallas_call x1, Pallas kernels, local(): pl.pallas_call(functools.partial(finish, total), out_shape=out_shape, in_...  4.43 us

profile of v3, /device:TPU:0, one launch (start us, length us, event | category | flops | bytes accessed | tf_op | source)
XLA Modules:
  0.0 45.1 jit_solution(14604928683995758646)
XLA Ops:
  0.6 40.0 %shard_map.221 = (f32[96,1536]{1,0:T(8,128)}, f32[2,1536]{1,0:T(2,128)}, f32[128,1536]{1,0:T(8,128)}) custom-call(f32[96,1536]{1,0:T(8,128)} %weight_ref.1, f32[96,1536]{1,0:T(8,128)} %tweight_ref.1, bf16[512,768]{1,0:T(8,128)(2,1)} %att_hbm.1, bf16[512,1536]{1,0:T(8,128)(2,1)} %cot_hbm.1, bf16[128,768]{1,0:T(8,128)(2,1)} %tatt_hbm.1), custom_call_target="tpu_custom_call" | custom-call | tf_op jit(solution)/shard_map/pallas_call | solution.py:554
  40.7 4.4 %shard_map.222 = (f32[96,1536]{1,0:T(8,128)}, f32[96,1536]{1,0:T(8,128)}, f32[96,1536]{1,0:T(8,128)}, f32[96,1536]{1,0:T(8,128)}, f32[96,1536]{1,0:T(8,128)}, /*...) custom-call(f32[96,1536]{1,0:T(8,128)} %get-tuple-element.14.grad_re, ...), custom_call_target="tpu_custom_call" | custom-call | tf_op jit(solution)/shard_map/pallas_call | solution.py:620
